TPU v7x, 256 devices: a whole 4x4x8 slice. The times are simulated.
256 devices in a mesh: ev: 4 (over z_hi, core), st: 64 (over x, z_lo, y).
Axes of the slice: x: 4, y: 4, z: 8 (z_hi: 2, z_lo: 4; z = z_hi * 4 + z_lo), core: 2. Of those that a mesh axis runs over, the one named last changes fastest.
Arguments:
- waveforms: bfloat16 [192, 512, 384], P('st', 'ev'), may hold values from -160 to 160
- availability: int32 [192, 512], P('st', 'ev'), may hold values 0 or 1
- lag_offset: int32 [192], P('st'), may hold values from -4 to 4
Outputs:
- correlation: float32 [17, 512, 512], P(None, ('ev', 'st'))
All inputs are finite; a program needn't handle non-finite values. No bound on the sum of `availability` on one device may be relied on, other than what follows from the above.
Results may differ from a plain program's by a relative error of at most 0.0024.
Values may be sent and summed in bfloat16 or wider, within the bound.
A program may use at most 128 MiB of HBM per device.

v0:
```python
import jax
import jax.numpy as jnp
from jax import lax
from jax.sharding import PartitionSpec as P

LAGS = 17
SHIFT_MOST = 4
epsilon = 1e-06


def normalize(waveforms, availability):
    wave_float = waveforms.astype(jnp.float32)
    energy = jnp.sum(wave_float * wave_float, axis=-1, keepdims=True)
    inverse_norm = availability.astype(jnp.float32)[..., None] * lax.rsqrt(energy + epsilon)
    return (wave_float * inverse_norm).astype(jnp.bfloat16)


def lag_stack(other_rows, shift_now):
    rows_other = other_rows.shape[0]
    samples = other_rows.shape[1] // 3
    pad_reach = SHIFT_MOST + (LAGS - 1) // 2
    split_rows = other_rows.reshape(rows_other, 3, samples)
    padded = jnp.pad(split_rows, ((0, 0), (0, 0), (pad_reach, pad_reach)))
    window = lax.dynamic_slice_in_dim(padded, SHIFT_MOST + shift_now, samples + LAGS - 1, 2)
    shifted = jnp.stack(
        [window[:, :, lag_index : lag_index + samples] for lag_index in range(LAGS)], 0
    )
    return shifted.reshape(LAGS, rows_other, 3 * samples)


def station_terms(own_block, other_block, offsets):
    shifted = jax.vmap(lag_stack)(other_block, offsets)
    return jnp.einsum("sik,sljk->lij", own_block, shifted, preferred_element_type=jnp.float32)


def on_device(waveforms, availability, lag_offset):
    unit_waves = normalize(waveforms, availability)
    ev_count = lax.axis_size("ev")
    ev_rows = unit_waves.shape[1]
    columns = ev_rows * ev_count
    gathered = lax.all_gather(unit_waves, "ev", axis=1, tiled=True)
    blocks = [
        (gathered[:, member * ev_rows : (member + 1) * ev_rows], jnp.int32(member * ev_rows))
        for member in range(ev_count)
    ]
    totals = jnp.zeros((LAGS, ev_rows, columns), jnp.float32)
    for other_block, first_col in blocks:
        partial_value = station_terms(unit_waves, other_block, lag_offset)
        totals = lax.dynamic_update_slice(totals, partial_value, (0, 0, first_col))
    return lax.psum_scatter(totals, "st", scatter_dimension=1, tiled=True)


def solution(mesh):
    placed = (P("st", "ev", None), P("st", "ev"), P("st"))
    return jax.shard_map(
        on_device,
        mesh=mesh,
        in_specs=placed,
        out_specs=P(None, ("ev", "st"), None),
        check_vma=False,
    )
```

profile of v0, /device:TPU:0, one launch (start us, length us, event | category | flops | bytes accessed | tf_op | source)
XLA Modules:
  0.0 487.4 jit_solution(12378270814222042738)
XLA Ops:
  6.5 1.2 copy.27
  7.8 0.7 rsqrt_multiply_fusion
  8.5 0.8 fusion.4
  9.3 0.7 fusion.78
  10.0 34.0 %all-gather.2.cloned.1.call-done = bf16[3,512,384]{1,2,0:T(8,128)(2,1)} async-done(((bf16[3,128,384]{1,2,0:T(8,128)(2,1)}), bf16[3,512,384]{1,2,0:T(8,128)(2,1)}) %all-gather.2.cloned.1.call-update) | async-done | bytes 1179664 | tf_op jit(solution)/shard_map/all_gather | solution.py:41
  44.0 1.3 fusion.79
  45.3 0.3 copy.28
  45.7 1.2 gather_fusion
  48.3 0.2 fusion.64
  48.4 0.2 fusion.63
  49.8 1.5 copy.29
  51.3 1.5 convolution_bitcast_fusion.3
  52.8 0.3 copy.32
  53.3 1.2 gather_fusion.1
  55.8 0.2 fusion.47
  57.4 3.7 copy.33
  61.0 0.3 copy.36
  61.5 1.3 gather_fusion.2
  64.2 0.2 fusion.30
  65.7 3.8 copy.37
  69.5 0.3 copy.40
  69.9 1.2 gather_fusion.3
  72.5 0.2 fusion.13
  74.0 3.4 copy-done.1
  77.4 4.5 copy.41
  82.0 2.5 dynamic_update_slice.12
  84.4 2.6 fusion.2
  87.0 2.8 fusion.1
  89.8 2.5 fusion
  92.3 6.2 %copy.44 = f32[17,128,512]{2,0,1:T(8,128)} copy(f32[17,128,512]{1,2,0:T(8,128)} %fusion) | data formatting | bytes 8912896 | tf_op jit(solution)/shard_map/dynamic_update_slice | solution.py:49
  98.6 380.4 %reduce-scatter.2.cloned.1.call-done = f32[17,2,512]{2,0,1:T(8,128)} async-done(((f32[17,128,512]{2,0,1:T(8,128)}), f32[17,2,512]{2,0,1:T(8,128)}) %reduce-scatter.2.cloned.1.call-update) | async-done | bytes 69648 | tf_op jit(solution)/shard_map/reduce_scatter | solution.py:50
  479.0 1.6 copy.45
  (85 shorter events, 11.6 us)
Async XLA Ops:
  6.5 37.4 %all-gather.2.cloned.1.call-start = ((), (), s32[]{:S(2)}) async-start(), calls=%async_computation.1 | async-start | bytes 1474560 | tf_op jit(solution)/shard_map/all_gather | solution.py:41
  9.3 469.7 %reduce-scatter.2.cloned.1.call-start = ((), (), s32[]{:S(2)}) async-start(), calls=%async_computation.2 | async-start | bytes 6389760 | tf_op jit(solution)/shard_map/reduce_scatter | solution.py:50
  49.5 1.8 copy-start
  73.9 10.6 %slice-start = ((s8[5013504]{0:T(1024)(128)(4,1)}), s8[4194304]{0:T(1024)(128)(4,1)S(1)}, s32[]{:S(2)}) async-start(s8[5013504]{0:T(1024)(128)(4,1)} %bitcast.330), calls=%async_computation.3 | async-start | bytes 8388608
  74.0 3.4 copy-start.1
  77.4 7.0 %slice-start.1 = ((s8[5013504]{0:T(1024)(128)(4,1)}), s8[819200]{0:T(1024)(128)(4,1)S(1)}, s32[]{:S(2)}) async-start(s8[5013504]{0:T(1024)(128)(4,1)} %bitcast.330), calls=%async_computation.4 | async-start | bytes 1638400
  77.4 9.6 %slice-start.2 = ((s8[5013504]{0:T(1024)(128)(4,1)}), s8[4194304]{0:T(1024)(128)(4,1)S(1)}, s32[]{:S(2)}) async-start(s8[5013504]{0:T(1024)(128)(4,1)} %bitcast.333), calls=%async_computation.5 | async-start | bytes 8388608
  81.9 5.1 %slice-start.3 = ((s8[5013504]{0:T(1024)(128)(4,1)}), s8[819200]{0:T(1024)(128)(4,1)S(1)}, s32[]{:S(2)}) async-start(s8[5013504]{0:T(1024)(128)(4,1)} %bitcast.333), calls=%async_computation.6 | async-start | bytes 1638400
Sparse Core Ops, SparseCore 0:
  9.4 34.5 all-gather.1
  98.7 380.2 reduce-scatter.1
where the time goes:
time: 488 us; the launch traced here: 487 us
  waiting for transfers between devices  414 us (85%)
  local copies, waits for them, and re-layouts  47.7 us (10%)
  between operations  13.6 us (3%)
  matrix products  9.43 us (2%)
    reduce_scatter x1, waiting for transfers between devices, on_device(): return lax.psum_scatter(totals, 'st', scatter_dimension=1, tiled=True)  380 us
    all_gather x1, waiting for transfers between devices, on_device(): gathered = lax.all_gather(unit_waves, 'ev', axis=1, tiled=True)  34 us
    unnamed x77, local copies, waits for them, and re-layouts  15.5 us
    transpose x4, local copies, waits for them, and re-layouts, lag_stack(): return shifted.reshape(LAGS, rows_other, 3 * samples)  13.4 us
  transfers between devices with their start and end apart: 2, of which 2 were waited for; matrix products, arithmetic and copies ran while one was open for 0% of the time, Pallas kernels for 0%

commit v1 on v0

--- a/solution.py
+++ b/solution.py
@@ -6,6 +6,13 @@
 LAGS = 17
 SHIFT_MOST = 4
 epsilon = 1e-06
+
+
+def supply_sample_on(u_in, on_dim):
+    z2 = jax.lax.all_to_all(
+        jnp.stack([u_in] * jax.lax.axis_size("ev"), axis=0), "ev", split_axis=0, concat_axis=0
+    )
+    return jnp.concatenate(z2, axis=on_dim)
 
 
 def normalize(waveforms, availability):
@@ -38,7 +45,7 @@
     ev_count = lax.axis_size("ev")
     ev_rows = unit_waves.shape[1]
     columns = ev_rows * ev_count
-    gathered = lax.all_gather(unit_waves, "ev", axis=1, tiled=True)
+    gathered = supply_sample_on(unit_waves, 1)
     blocks = [
         (gathered[:, member * ev_rows : (member + 1) * ev_rows], jnp.int32(member * ev_rows))
         for member in range(ev_count)

time: 488 us -> 494 us (1.012)
  starting transfers between devices: 0.04 us -> 6.72 us
    all_gather x1 -> x0, waiting for transfers between devices: 34 us -> none  [on_device(): gathered = lax.all_gather(unit_waves, 'ev', axis=1, tiled=True)]
    all_to_all x0 -> x1, waiting for transfers between devices: none -> 30.9 us  [supply_sample_on(): jax.lax.all_to_all(jnp.stack([u_in] * jax.lax.axis_size('ev'), axis=0), '...]
    all_to_all x0 -> x1, starting transfers between devices: none -> 6.72 us  [supply_sample_on(): jax.lax.all_to_all(jnp.stack([u_in] * jax.lax.axis_size('ev'), axis=0), '...]
    unnamed x77 -> x74, local copies, waits for them, and re-layouts: 15.5 us -> 14.4 us
where the time goes in v1:
time: 494 us
  waiting for transfers between devices  413 us (84%)
  local copies, waits for them, and re-layouts  47.5 us (10%)
  between operations  13.6 us (3%)
  matrix products  9.36 us (2%)
  starting transfers between devices  6.72 us (1%)
    reduce_scatter x1, waiting for transfers between devices, on_device(): return lax.psum_scatter(totals, 'st', scatter_dimension=1, tiled=True)  382 us
    all_to_all x1, waiting for transfers between devices, supply_sample_on(): jax.lax.all_to_all(jnp.stack([u_in] * jax.lax.axis_size('ev'), axis=0), '...  30.9 us
    unnamed x74, local copies, waits for them, and re-layouts  14.4 us
    transpose x4, local copies, waits for them, and re-layouts, lag_stack(): return shifted.reshape(LAGS, rows_other, 3 * samples)  13.4 us
  transfers between devices with their start and end apart: 2, of which 2 were waited for; matrix products, arithmetic and copies ran while one was open for 0% of the time, Pallas kernels for 0%

profile of v1, /device:TPU:0, one launch (start us, length us, event | category | flops | bytes accessed | tf_op | source)
XLA Modules:
  0.0 494.0 jit_solution(3484445403509683217)
XLA Ops:
  6.5 1.1 fusion.3
  7.6 0.7 rsqrt_multiply_fusion
  8.3 1.1 fusion.4
  9.4 1.2 stack.223
  10.6 6.7 %all-to-all-start = ((bf16[4,3,128,384]{3,2,1,0:T(8,128)(2,1)}), bf16[4,3,128,384]{3,2,1,0:T(8,128)(2,1)S(1)}, u32[]{:S(2)}, u32[]{:S(2)}) async-start(bf16[4,3,128,384]{3,2,1,0:T(8,128)(2,1)} %stack.223), calls=%async_computation | async-start | bytes 2359296 | tf_op jit(solution)/shard_map/all_to_all | solution.py:12
  17.3 0.7 fusion.78
  18.0 30.9 %all-to-all-done = bf16[4,3,128,384]{3,2,1,0:T(8,128)(2,1)S(1)} async-done(((bf16[4,3,128,384]{3,2,1,0:T(8,128)(2,1)}), bf16[4,3,128,384]{3,2,1,0:T(8,128)(2,1)S(1)}, u32[]{:S(2)}, u32[]{:S(2)}) %all-to-all-start) | async-done | bytes 1179680 | tf_op jit(solution)/shard_map/all_to_all | solution.py:12
  49.1 0.2 copy.27
  49.4 0.3 copy.28
  49.8 1.2 gather_fusion
  53.9 1.5 copy.29
  55.3 1.5 convolution_bitcast_fusion.3
  56.9 0.2 copy.31
  57.1 0.3 copy.32
  57.5 1.2 gather_fusion.1
  61.6 3.7 copy.33
  65.3 0.2 copy.35
  65.5 0.4 copy.36
  66.1 1.2 gather_fusion.2
  70.2 3.8 copy.37
  74.0 0.2 copy.39
  74.2 0.3 copy.40
  74.7 1.2 gather_fusion.3
  78.8 3.4 copy-done
  82.2 4.5 copy.41
  86.7 2.5 dynamic_update_slice.12
  89.2 2.5 fusion.2
  91.7 2.7 fusion.1
  94.4 2.5 fusion
  97.0 6.2 %copy.43 = f32[17,128,512]{2,0,1:T(8,128)} copy(f32[17,128,512]{1,2,0:T(8,128)} %fusion) | data formatting | bytes 8912896 | tf_op jit(solution)/shard_map/dynamic_update_slice | solution.py:56
  103.2 382.3 %reduce-scatter.2.cloned.1.call-done = f32[17,2,512]{2,0,1:T(8,128)} async-done(((f32[17,128,512]{2,0,1:T(8,128)}), f32[17,2,512]{2,0,1:T(8,128)}) %reduce-scatter.2.cloned.1.call-update) | async-done | bytes 69648 | tf_op jit(solution)/shard_map/reduce_scatter | solution.py:57
  485.6 1.6 copy.44
  (87 shorter events, 12.6 us)
Async XLA Ops:
  10.6 38.3 %all-to-all-start = ((bf16[4,3,128,384]{3,2,1,0:T(8,128)(2,1)}), bf16[4,3,128,384]{3,2,1,0:T(8,128)(2,1)S(1)}, u32[]{:S(2)}, u32[]{:S(2)}) async-start(bf16[4,3,128,384]{3,2,1,0:T(8,128)(2,1)} %stack.223), calls=%async_computation | async-start | bytes 2359296 | tf_op jit(solution)/shard_map/all_to_all | solution.py:12
  17.3 468.3 %reduce-scatter.2.cloned.1.call-start = ((), (), s32[]{:S(2)}) async-start(), calls=%async_computation.2 | async-start | bytes 6389760 | tf_op jit(solution)/shard_map/reduce_scatter | solution.py:57
  78.6 10.6 %slice-start = ((s8[5013504]{0:T(1024)(128)(4,1)}), s8[4194304]{0:T(1024)(128)(4,1)S(1)}, s32[]{:S(2)}) async-start(s8[5013504]{0:T(1024)(128)(4,1)} %bitcast.330), calls=%async_computation.3 | async-start | bytes 8388608
  78.8 3.4 copy-start
  82.1 7.0 %slice-start.1 = ((s8[5013504]{0:T(1024)(128)(4,1)}), s8[819200]{0:T(1024)(128)(4,1)S(1)}, s32[]{:S(2)}) async-start(s8[5013504]{0:T(1024)(128)(4,1)} %bitcast.330), calls=%async_computation.4 | async-start | bytes 1638400
  82.1 9.5 %slice-start.2 = ((s8[5013504]{0:T(1024)(128)(4,1)}), s8[4194304]{0:T(1024)(128)(4,1)S(1)}, s32[]{:S(2)}) async-start(s8[5013504]{0:T(1024)(128)(4,1)} %bitcast.333), calls=%async_computation.5 | async-start | bytes 8388608
  86.7 5.0 %slice-start.3 = ((s8[5013504]{0:T(1024)(128)(4,1)}), s8[819200]{0:T(1024)(128)(4,1)S(1)}, s32[]{:S(2)}) async-start(s8[5013504]{0:T(1024)(128)(4,1)} %bitcast.333), calls=%async_computation.6 | async-start | bytes 1638400
Sparse Core Ops, SparseCore 0:
  103.4 382.1 reduce-scatter.1
